TPU v7x, 32 devices: a whole 2x2x4 slice. The times are simulated.
32 devices in a mesh: outer: 4 (over x, core), inner: 8 (over z, y).
Axes of the slice: x: 2, y: 2, z: 4, core: 2. Of those that a mesh axis runs over, the one named last changes fastest.
Arguments:
- projected: bfloat16 [4096, 12288], P(('outer', 'inner')), may hold values from -6 to 6
- short_filter: bfloat16 [3, 12288], replicated, may hold values from -3.5 to 3.5
- long_filter: bfloat16 [4096, 4096], P(('outer', 'inner')), may hold values from 0 to 0.35
- skip: float32 [4096], replicated, may hold values from 0.1 to 1.9
Outputs:
- mixed: bfloat16 [4096, 4096], P(('outer', 'inner'))
All inputs are finite; a program needn't handle non-finite values.
Results may differ from a plain program's by a relative error of at most 0.0075.
Values may be sent and summed in bfloat16 or wider, within the bound.
A program may use at most 128 MiB of HBM per device.

v0:
```python
import functools
import math

import jax
import jax.numpy as jnp
import numpy as np
from jax import lax
from jax.experimental import pallas as pl
from jax.experimental.pallas import tpu as pltpu
from jax.sharding import PartitionSpec as P

TWO_PI = 2.0 * math.pi
MESH = pl.DeviceIdType.MESH
LANES = 128
ROWS = 16
RADIX = 8


class Cx:
    def __init__(self, re, im=None):
        self.re, self.im = re, im

    def __add__(self, other):
        if self.im is None:
            im = other.im
        elif other.im is None:
            im = self.im
        else:
            im = self.im + other.im
        return Cx(self.re + other.re, im)

    def __sub__(self, other):
        if other.im is None:
            im = self.im
        elif self.im is None:
            im = -other.im
        else:
            im = self.im - other.im
        return Cx(self.re - other.re, im)

    def conj(self):
        return Cx(self.re, None if self.im is None else -self.im)

    def times(self, turns, length):
        turns = turns % length
        if turns == 0:
            return self
        if 2 * turns == length:
            return Cx(-self.re, None if self.im is None else -self.im)
        cos, sin = math.cos(TWO_PI * turns / length), math.sin(TWO_PI * turns / length)
        if self.im is None:
            return Cx(self.re * cos, self.re * sin)
        if 8 * turns % length == 0 and 4 * turns % length != 0:
            half = math.sqrt(0.5)
            one, two = self.re * half, self.im * half
            signs = (round(cos / half), round(sin / half))
            re = {(1, 1): one - two, (1, -1): one + two, (-1, 1): -(one + two), (-1, -1): two - one}
            im = {(1, 1): one + two, (1, -1): two - one, (-1, 1): one - two, (-1, -1): -(one + two)}
            return Cx(re[signs], im[signs])
        return Cx(self.re * cos - self.im * sin, self.re * sin + self.im * cos)

    def plus_i(self, other, sign):
        if other.im is None:
            re = self.re
        else:
            re = self.re - other.im if sign > 0 else self.re + other.im
        turned = other.re if sign > 0 else -other.re
        return Cx(re, turned if self.im is None else self.im + turned)


def dft4(z, sign):
    s, t, u, v = z[0] + z[2], z[0] - z[2], z[1] + z[3], z[1] - z[3]
    return [s + u, t.plus_i(v, sign), s - u, t.plus_i(v, -sign)]


def dft8(z, sign):
    even, odd = dft4(z[0::2], sign), dft4(z[1::2], sign)
    out = [None] * 8
    for k in range(4):
        if k == 2:
            out[2], out[6] = even[2].plus_i(odd[2], sign), even[2].plus_i(odd[2], -sign)
        else:
            turned = odd[k].times(sign * k, 8)
            out[k], out[k + 4] = even[k] + turned, even[k] - turned
    return out


def forward64(x):
    half = math.sqrt(0.5)
    first = [[None] * 8 for _ in range(5)]
    for b in range(8):
        x0, x1, x2, x3 = x[b], x[b + 8], x[b + 16], x[b + 24]
        p, q, d = x0 + x2, x1 + x3, x1 - x3
        e, f = q * half, d * half
        first[0][b] = Cx(p + q)
        first[4][b] = Cx(p - q)
        first[2][b] = Cx(x0 - x2, -d)
        first[1][b] = Cx(x0 + f, -(e + x2))
        first[3][b] = Cx(x0 - f, x2 - e)
    out = {}
    for k1 in range(5):
        done = dft8([first[k1][b].times(-b * k1, 64) for b in range(8)], -1)
        for k0 in range(8):
            freq = k1 + 8 * k0
            if freq <= 32:
                out[freq] = done[k0]
            elif k1 not in (0, 4):
                out[64 - freq] = done[k0].conj()
    return out


def backward64(spec):
    half = math.sqrt(0.5)
    held = [None] * 5
    for k1 in range(5):
        values = []
        for k0 in range(8):
            freq = k1 + 8 * k0
            values.append(spec[freq] if freq <= 32 else spec[64 - freq].conj())
        done = dft8(values, 1)
        held[k1] = [done[b].times(b * k1, 64) for b in range(8)]
    out = [None] * 32
    for b in range(8):
        h0, h4 = held[0][b].re, held[4][b].re
        h1, h2, h3 = held[1][b], held[2][b], held[3][b]
        plus, minus = h0 + h4, h0 - h4
        a1, a3 = (h1.re - h3.re), (h1.im + h3.im)
        out[b] = plus + 2.0 * (h1.re + h2.re + h3.re)
        out[b + 16] = plus + 2.0 * (h3.im - h1.im - h2.re)
        out[b + 8] = minus + 2.0 * (half * (a1 - a3) - h2.im)
        out[b + 24] = minus + 2.0 * (h2.im - half * (a1 + a3))
    return out


def kernel(
    n, n_inner, proj_hbm, filt_hbm, taps_ref, skip_ref, fwd_ref, bwd_ref, turn_ref, out_ref,
    proj, halo, filt_in, gate_in, gate_out, conv_out, conv_in, first, fspec, back, turn, query,
    proj_sem, own_sem, halo_send, halo_recv, f_send, f_recv, g_send, g_recv, y_send, y_recv,
):
    tok = proj.shape[0]
    width = filt_hbm.shape[1]
    freqs = first.shape[0]
    outer, inner = lax.axis_index("outer"), lax.axis_index("inner")
    me = outer * n_inner + inner

    def place(device):
        return (device // n_inner, device % n_inner)

    def partner(step):
        return lax.rem(me + step, n)

    def columns(block, part=0):
        return pl.ds(pl.multiple_of(part * width + block * LANES, LANES), LANES)

    def each_partner(body):
        def run(step, carry):
            body(partner(step))
            return carry
        lax.fori_loop(1, n, run, 0)

    def halo_copy(to):
        return pltpu.make_async_remote_copy(
            src_ref=proj_hbm.at[pl.ds(tok - ROWS, ROWS), :], dst_ref=halo,
            send_sem=halo_send, recv_sem=halo_recv, device_id=place(to), device_id_type=MESH,
        )

    def filter_copy(to, slot, sem):
        return pltpu.make_async_remote_copy(
            src_ref=filt_hbm.at[:, columns(to)], dst_ref=filt_in.at[slot],
            send_sem=f_send.at[to], recv_sem=f_recv.at[sem], device_id=place(to), device_id_type=MESH,
        )

    def gate_copy(to, slot, sem):
        return pltpu.make_async_remote_copy(
            src_ref=gate_out.at[to], dst_ref=gate_in.at[slot],
            send_sem=g_send.at[to], recv_sem=g_recv.at[sem], device_id=place(to), device_id_type=MESH,
        )

    def conv_copy(to, slot, sem):
        return pltpu.make_async_remote_copy(
            src_ref=conv_out.at[to], dst_ref=conv_in.at[slot],
            send_sem=y_send.at[to], recv_sem=y_recv.at[sem], device_id=place(to), device_id_type=MESH,
        )

    load = pltpu.make_async_copy(proj_hbm, proj, proj_sem)
    load.start()
    own = pltpu.make_async_copy(filt_hbm.at[:, columns(me)], filt_in.at[me], own_sem)
    own.start()

    barrier = pltpu.get_barrier_semaphore()
    each_partner(lambda to: pl.semaphore_signal(
        barrier, inc=1, device_id=place(to), device_id_type=MESH))
    pl.semaphore_wait(barrier, n - 1)

    @pl.when(me < n - 1)
    def _():
        halo_copy(me + 1).start()

    each_partner(lambda to: filter_copy(to, me, me).start())

    load.wait()

    @pl.when(me == 0)
    def _():
        halo[...] = jnp.zeros_like(halo)

    @pl.when(me > 0)
    def _():
        halo_copy(me).wait_recv()

    def featured(block, part):
        cols = columns(block, part)
        taps = taps_ref[:, cols].astype(jnp.float32)
        rows = jnp.concatenate(
            [halo[:, cols].astype(jnp.float32), proj[:, cols].astype(jnp.float32)], 0)
        count = taps.shape[0]
        total = None
        for tap in range(count):
            start = ROWS - tap
            term = taps[tap:tap + 1] * rows[start:start + tok]
            total = term if total is None else total + term
        return total

    def gate(block):
        return (featured(block, 1) * featured(block, 2)).astype(jnp.bfloat16)

    def send_gate(to):
        gate_out[to] = gate(to)
        gate_copy(to, me, me).start()

    each_partner(send_gate)
    own_gate = gate(me)
    gate_out[me] = own_gate
    gate_in[me] = own_gate

    for freq in range(freqs):
        for part in range(2):
            turn[freq, part] = jnp.broadcast_to(
                turn_ref[part][:, freq:freq + 1], (tok, LANES))

    def ask(block, carry):
        query[block] = featured(block, 0)
        return carry

    lax.fori_loop(0, n, ask, 0)

    def first_section(source):
        def run(tile, carry):
            rows = pl.ds(pl.multiple_of(tile * ROWS, ROWS), ROWS)
            low = pl.ds(pl.multiple_of(tok + tile * ROWS, ROWS), ROWS)
            spec = forward64([source[b, rows, :].astype(jnp.float32) for b in range(n)])
            for freq in range(freqs):
                cos, sin = turn[freq, 0, rows, :], turn[freq, 1, rows, :]
                z = spec[freq]
                if z.im is None:
                    re, im = z.re * cos, -(z.re * sin)
                else:
                    re, im = z.re * cos + z.im * sin, z.im * cos - z.re * sin
                first[freq, rows, :] = re.astype(jnp.bfloat16)
                first[freq, low, :] = im.astype(jnp.bfloat16)
            return carry
        lax.fori_loop(0, tok // ROWS, run, 0)

    own.wait()
    each_partner(lambda src: filter_copy(src, src, src).wait_recv())
    first_section(filt_in)

    def filter_spectrum(freq, carry):
        fspec[freq] = jnp.dot(fwd_ref[...], first[freq], preferred_element_type=jnp.float32)
        return carry

    lax.fori_loop(0, freqs, filter_spectrum, 0)

    each_partner(lambda src: gate_copy(src, src, src).wait_recv())
    first_section(gate_in)

    def through(freq, carry):
        spec = jnp.dot(fwd_ref[...], first[freq], preferred_element_type=jnp.float32)
        sr, si = spec[:tok], spec[tok:]
        fr, fi = fspec[freq, :tok], fspec[freq, tok:]
        product = jnp.concatenate([sr * fr - si * fi, sr * fi + si * fr], 0).astype(jnp.bfloat16)
        result = jnp.dot(bwd_ref[...], product, preferred_element_type=jnp.float32)
        br, bi = result[:tok], result[tok:]
        cos, sin = turn[freq, 0], turn[freq, 1]
        back[freq, :tok] = br * cos - bi * sin
        back[freq, tok:] = bi * cos + br * sin
        return carry

    lax.fori_loop(0, freqs, through, 0)

    scale = 1.0 / (2 * n * tok)

    def last_section(tile, carry):
        rows = pl.ds(pl.multiple_of(tile * ROWS, ROWS), ROWS)
        low = pl.ds(pl.multiple_of(tok + tile * ROWS, ROWS), ROWS)
        done = backward64([Cx(back[freq, rows, :], back[freq, low, :]) for freq in range(freqs)])
        for b in range(n):
            conv_out[b, rows, :] = (done[b] * scale).astype(jnp.bfloat16)
        return carry

    lax.fori_loop(0, tok // ROWS, last_section, 0)

    each_partner(lambda to: conv_copy(to, me, me).start())

    def finish(block, rows):
        cols = columns(block)
        mixed = query[block] * (
            rows.astype(jnp.float32) + skip_ref[:, cols] * gate_out[block].astype(jnp.float32))
        out_ref[:, cols] = mixed.astype(jnp.bfloat16)

    finish(me, conv_out[me])

    def take(src):
        conv_copy(src, src, src).wait_recv()
        finish(src, conv_in[src])

    each_partner(take)

    @pl.when(me < n - 1)
    def _():
        halo_copy(me + 1).wait_send()

    def sent(to):
        filter_copy(to, me, me).wait_send()
        gate_copy(to, me, me).wait_send()
        conv_copy(to, me, me).wait_send()

    each_partner(sent)


def cosines(rows, cols, length):
    angle = (np.arange(rows)[:, None] * np.arange(cols)[None, :] % length) * (TWO_PI / length)
    return np.cos(angle), np.sin(angle)


def by_channels(projected, short_filter, long_filter, skip):
    n_inner = lax.axis_size("inner")
    n = lax.axis_size("outer") * n_inner
    tok, width = long_filter.shape
    freqs = n + 1
    cos, sin = cosines(tok, tok, tok)
    forward = np.block([[cos, sin], [-sin, cos]]).astype(jnp.bfloat16)
    backward = np.block([[cos, -sin], [sin, cos]]).astype(jnp.bfloat16)
    turns = np.stack(cosines(tok, LANES, 2 * n * tok)).astype(np.float32)
    vmem = pl.BlockSpec(memory_space=pltpu.VMEM)
    hbm = pl.BlockSpec(memory_space=pl.ANY)
    block = (n, tok, LANES)
    dma = pltpu.SemaphoreType.DMA
    return pl.pallas_call(
        functools.partial(kernel, n, n_inner),
        out_shape=jax.ShapeDtypeStruct((tok, width), jnp.bfloat16),
        in_specs=[hbm, hbm] + [vmem] * 5,
        out_specs=vmem,
        scratch_shapes=[
            pltpu.VMEM(projected.shape, jnp.bfloat16),
            pltpu.VMEM((ROWS, projected.shape[1]), jnp.bfloat16),
            pltpu.VMEM(block, jnp.bfloat16),
            pltpu.VMEM(block, jnp.bfloat16),
            pltpu.VMEM(block, jnp.bfloat16),
            pltpu.VMEM(block, jnp.bfloat16),
            pltpu.VMEM(block, jnp.bfloat16),
            pltpu.VMEM((freqs, 2 * tok, LANES), jnp.bfloat16),
            pltpu.VMEM((freqs, 2 * tok, LANES), jnp.float32),
            pltpu.VMEM((freqs, 2 * tok, LANES), jnp.float32),
            pltpu.VMEM((freqs, 2, tok, LANES), jnp.float32),
            pltpu.VMEM(block, jnp.float32),
            dma, dma, dma, dma,
            dma((n,)), dma((n,)), dma((n,)), dma((n,)), dma((n,)), dma((n,)),
        ],
        compiler_params=pltpu.CompilerParams(
            collective_id=0, has_side_effects=True, vmem_limit_bytes=56 * 1024 * 1024),
        cost_estimate=pl.CostEstimate(
            flops=2 * 3 * freqs * (2 * tok) ** 2 * LANES,
            bytes_accessed=10 * tok * width, transcendentals=0),
    )(projected, long_filter, short_filter, skip[None, :],
      jnp.asarray(forward), jnp.asarray(backward), jnp.asarray(turns))


def passed_along(value, axis, by):
    length = lax.axis_size(axis)
    pairs = [(i, i + by) for i in range(length) if 0 <= i + by < length]
    return lax.ppermute(value, axis, pairs)


def turn_table(rows, cols, length):
    product = rows * cols % length
    angle = product.astype(jnp.float32) * (TWO_PI / length)
    return (jnp.cos(angle), jnp.sin(angle))


def counting(count):
    return jnp.arange(count, dtype=jnp.int32)


def narrowed(table_pair):
    return (table_pair[0].astype(jnp.bfloat16), table_pair[1].astype(jnp.bfloat16))


def contract(form, table, values):
    return jnp.einsum(form, table, values, preferred_element_type=jnp.float32)


def shards(projected, short_filter, long_filter, skip):
    outer_count = lax.axis_size("outer")
    inner_count = lax.axis_size("inner")
    segments = outer_count * inner_count
    tok_rows, width_cols = long_filter.shape
    local_rows = tok_rows // segments
    freq_rows = 2 * segments
    freq_local = 2
    transform = freq_rows * tok_rows
    position = lax.axis_index(("outer", "inner"))
    tap_count = short_filter.shape[0]
    rim_count = tap_count - 1
    previous_rows = passed_along(projected[tok_rows - rim_count :], ("outer", "inner"), 1)
    extended = jnp.concatenate([previous_rows, projected], 0)
    featured = jnp.zeros(projected.shape, jnp.float32)
    for tap_index in range(tap_count):
        offset = rim_count - tap_index
        featured = featured + short_filter[tap_index].astype(jnp.float32) * extended[
            offset : offset + tok_rows
        ].astype(jnp.float32)
    query_rows = featured[:, :width_cols]
    gated_rows = (featured[:, width_cols : 2 * width_cols] * featured[:, 2 * width_cols :]).astype(
        jnp.bfloat16
    )
    cos_first, sin_first = narrowed(
        turn_table(counting(freq_rows)[:, None], counting(segments)[None, :], freq_rows)
    )
    owned_rows = position * local_rows + counting(local_rows)
    turn_cos, turn_sin = turn_table(counting(freq_rows)[:, None], owned_rows[None, :], transform)
    turn_cos = turn_cos[:, :, None]
    turn_sin = turn_sin[:, :, None]
    cos_local, sin_local = narrowed(
        turn_table(counting(tok_rows)[:, None], counting(tok_rows)[None, :], tok_rows)
    )
    owned_freqs = position * freq_local + counting(freq_local)
    back_cos, back_sin = turn_table(owned_freqs[:, None], counting(tok_rows)[None, :], transform)
    back_cos = back_cos[:, :, None]
    back_sin = back_sin[:, :, None]
    cos_last, sin_last = narrowed(
        turn_table(counting(segments)[:, None], counting(freq_rows)[None, :], freq_rows)
    )

    def first_section(stacked):
        real_part = contract("kb,bac->kac", cos_first, stacked)
        imag_part = -contract("kb,bac->kac", sin_first, stacked)
        out_real = (real_part * turn_cos + imag_part * turn_sin).astype(jnp.bfloat16)
        out_imag = (imag_part * turn_cos - real_part * turn_sin).astype(jnp.bfloat16)
        return (out_real, out_imag)

    def forward_local(real_half, imag_half):
        spec_real = contract("ua,kac->kuc", cos_local, real_half) + contract(
            "ua,kac->kuc", sin_local, imag_half
        )
        spec_imag = contract("ua,kac->kuc", cos_local, imag_half) - contract(
            "ua,kac->kuc", sin_local, real_half
        )
        return (spec_real, spec_imag)

    moved = (
        lax.all_to_all(
            gated_rows.reshape(segments, local_rows, width_cols),
            ("outer", "inner"),
            split_axis=0,
            concat_axis=0,
            tiled=True,
        ),
        lax.all_to_all(
            long_filter.reshape(segments, local_rows, width_cols),
            ("outer", "inner"),
            split_axis=0,
            concat_axis=0,
            tiled=True,
        ),
    )
    signal_cols = moved[0]
    filter_cols = moved[1]
    signal_real, signal_imag = first_section(signal_cols)
    filter_real, filter_imag = first_section(filter_cols)
    spectral_pieces = (
        lax.all_to_all(signal_real, ("outer", "inner"), split_axis=0, concat_axis=1, tiled=True),
        lax.all_to_all(signal_imag, ("outer", "inner"), split_axis=0, concat_axis=1, tiled=True),
        lax.all_to_all(filter_real, ("outer", "inner"), split_axis=0, concat_axis=1, tiled=True),
        lax.all_to_all(filter_imag, ("outer", "inner"), split_axis=0, concat_axis=1, tiled=True),
    )
    signal_real, signal_imag = forward_local(spectral_pieces[0], spectral_pieces[1])
    filter_real, filter_imag = forward_local(spectral_pieces[2], spectral_pieces[3])
    product_real = (signal_real * filter_real - signal_imag * filter_imag).astype(jnp.bfloat16)
    product_imag = (signal_real * filter_imag + signal_imag * filter_real).astype(jnp.bfloat16)
    back_real = contract("au,kuc->kac", cos_local, product_real) - contract(
        "au,kuc->kac", sin_local, product_imag
    )
    back_imag = contract("au,kuc->kac", cos_local, product_imag) + contract(
        "au,kuc->kac", sin_local, product_real
    )
    out_real = (back_real * back_cos - back_imag * back_sin).astype(jnp.bfloat16)
    out_imag = (back_imag * back_cos + back_real * back_sin).astype(jnp.bfloat16)
    moved = (
        lax.all_to_all(out_real, ("outer", "inner"), split_axis=1, concat_axis=0, tiled=True),
        lax.all_to_all(out_imag, ("outer", "inner"), split_axis=1, concat_axis=0, tiled=True),
    )
    rows_real = moved[0]
    rows_imag = moved[1]
    long_conv = (
        contract("bk,kac->bac", cos_last, rows_real) - contract("bk,kac->bac", sin_last, rows_imag)
    ) * (1.0 / transform)
    moved = lax.all_to_all(
        long_conv.astype(jnp.bfloat16), ("outer", "inner"), split_axis=0, concat_axis=0, tiled=True
    )
    conv_rows = moved.reshape(tok_rows, width_cols)
    mixed = query_rows * (
        conv_rows.astype(jnp.float32) + skip[None, :] * gated_rows.astype(jnp.float32)
    )
    return mixed.astype(jnp.bfloat16)


def operator(projected, short_filter, long_filter, skip):
    segments = lax.axis_size("outer") * lax.axis_size("inner")
    tok_rows, width_cols = long_filter.shape
    if 2 * segments == RADIX * RADIX and tok_rows == LANES and width_cols == segments * LANES:
        return by_channels(projected, short_filter, long_filter, skip)
    return shards(projected, short_filter, long_filter, skip)


def solution(mesh):
    in_specs = (P(("outer", "inner"), None), P(), P(("outer", "inner"), None), P())
    out_specs = P(("outer", "inner"), None)
    return jax.shard_map(operator, mesh=mesh, in_specs=in_specs, out_specs=out_specs, check_vma=False)
```

profile of v0, /device:TPU:1, one launch (start us, length us, event | category | flops | bytes accessed | tf_op | source)
XLA Modules:
  0.0 108.9 jit_solution(2446525771562578444)
XLA Ops:
  0.0 106.6 %shard_map.73 = bf16[128,4096]{1,0:T(8,128)(2,1)} custom-call(bf16[128,12288]{1,0:T(8,128)(2,1)} %proj_hbm.1, bf16[128,4096]{1,0:T(8,128)(2,1)} %filt_hbm.1, bf16[3,12288]{1,0:T(4,128)(2,1)} %taps_ref.1, f32[1,4096]{1,0:T(1,128)} %bitcast.1, bf16[256,256]{1,0:T(8,128)(2,1)} %constant.6.clone.fwd_ref, bf16[256,256]{1,0:T(8,128)(2,1)} %constant.7.clone.bwd_ref, ...), custom_call_target="tpu_custom_call" | custom-call | flops 1660944384 | bytes 5242880 | tf_op jit(solution)/shard_map/pallas_call | solution.py:349
  106.6 2.3 %copy.9 = bf16[128,4096]{1,0:T(8,128)(2,1)} copy(bf16[128,4096]{1,0:T(8,128)(2,1)} %shard_map.73) | data formatting | bytes 2097152
where the time goes:
time: 109 us
  Pallas kernels  107 us (98%)
  local copies, waits for them, and re-layouts  2.29 us (2%)
    pallas_call x1, Pallas kernels, by_channels(): pl.pallas_call(functools.partial(kernel, n, n_inner), out_shape=jax.Shape...  107 us
    unnamed x1, local copies, waits for them, and re-layouts  2.29 us

commit v1 on v0

--- a/solution.py
+++ b/solution.py
@@ -12,6 +12,7 @@
 TWO_PI = 2.0 * math.pi
 MESH = pl.DeviceIdType.MESH
 LANES = 128
+HALF = LANES // 2
 ROWS = 16
 RADIX = 8
 
@@ -132,31 +133,44 @@
     return out
 
 
+def swapped_halves(x, y):
+    left = lax.broadcasted_iota(jnp.int32, x.shape, 1) < HALF
+    return (
+        jnp.where(left, x, pltpu.roll(y, HALF, 1)),
+        jnp.where(left, pltpu.roll(x, HALF, 1), y),
+    )
+
+
 def kernel(
     n, n_inner, proj_hbm, filt_hbm, taps_ref, skip_ref, fwd_ref, bwd_ref, turn_ref, out_ref,
-    proj, halo, filt_in, gate_in, gate_out, conv_out, conv_in, first, fspec, back, turn, query,
-    proj_sem, own_sem, halo_send, halo_recv, f_send, f_recv, g_send, g_recv, y_send, y_recv,
+    proj, filt, halo, filt_out, gate_out, conv_out, filt_in, gate_in, conv_in,
+    gated, first, fspec, back, turn, query,
+    proj_sem, filt_sem, halo_send, halo_recv, f_send, f_recv, g_send, g_recv, y_send, y_recv,
 ):
-    tok = proj.shape[0]
-    width = filt_hbm.shape[1]
-    freqs = first.shape[0]
+    tok, width = filt.shape
+    freqs = n + 1
+    half_tok = tok // 2
+    quads = first.shape[0]
     outer, inner = lax.axis_index("outer"), lax.axis_index("inner")
     me = outer * n_inner + inner
 
     def place(device):
         return (device // n_inner, device % n_inner)
 
-    def partner(step):
-        return lax.rem(me + step, n)
-
     def columns(block, part=0):
         return pl.ds(pl.multiple_of(part * width + block * LANES, LANES), LANES)
 
     def each_partner(body):
         def run(step, carry):
-            body(partner(step))
+            body(lax.rem(me + step, n))
             return carry
         lax.fori_loop(1, n, run, 0)
+
+    def loop(count, body):
+        def run(step, carry):
+            body(step)
+            return carry
+        lax.fori_loop(0, count, run, 0)
 
     def halo_copy(to):
         return pltpu.make_async_remote_copy(
@@ -164,39 +178,51 @@
             send_sem=halo_send, recv_sem=halo_recv, device_id=place(to), device_id_type=MESH,
         )
 
-    def filter_copy(to, slot, sem):
+    def chunk_copy(source, target, send, recv, half, to, slot):
         return pltpu.make_async_remote_copy(
-            src_ref=filt_hbm.at[:, columns(to)], dst_ref=filt_in.at[slot],
-            send_sem=f_send.at[to], recv_sem=f_recv.at[sem], device_id=place(to), device_id_type=MESH,
+            src_ref=source.at[half, to], dst_ref=target.at[half, slot],
+            send_sem=send.at[half, to], recv_sem=recv.at[half, slot],
+            device_id=place(to), device_id_type=MESH,
         )
 
-    def gate_copy(to, slot, sem):
-        return pltpu.make_async_remote_copy(
-            src_ref=gate_out.at[to], dst_ref=gate_in.at[slot],
-            send_sem=g_send.at[to], recv_sem=g_recv.at[sem], device_id=place(to), device_id_type=MESH,
-        )
-
-    def conv_copy(to, slot, sem):
-        return pltpu.make_async_remote_copy(
-            src_ref=conv_out.at[to], dst_ref=conv_in.at[slot],
-            send_sem=y_send.at[to], recv_sem=y_recv.at[sem], device_id=place(to), device_id_type=MESH,
-        )
-
+    filter_copy = functools.partial(chunk_copy, filt_out, filt_in, f_send, f_recv)
+    gate_copy = functools.partial(chunk_copy, gate_out, gate_in, g_send, g_recv)
+    conv_copy = functools.partial(chunk_copy, conv_out, conv_in, y_send, y_recv)
+
+    def send_all(copy, half):
+        each_partner(lambda to: copy(half, to, me).start())
+
+    def receive_all(copy, half):
+        each_partner(lambda src: copy(half, src, src).wait_recv())
+
+    load_filt = pltpu.make_async_copy(filt_hbm, filt, filt_sem)
+    load_filt.start()
     load = pltpu.make_async_copy(proj_hbm, proj, proj_sem)
     load.start()
-    own = pltpu.make_async_copy(filt_hbm.at[:, columns(me)], filt_in.at[me], own_sem)
-    own.start()
 
     barrier = pltpu.get_barrier_semaphore()
     each_partner(lambda to: pl.semaphore_signal(
         barrier, inc=1, device_id=place(to), device_id_type=MESH))
+    load_filt.wait()
     pl.semaphore_wait(barrier, n - 1)
 
     @pl.when(me < n - 1)
     def _():
         halo_copy(me + 1).start()
 
-    each_partner(lambda to: filter_copy(to, me, me).start())
+    def packed(values):
+        first_half, second_half = swapped_halves(values[:half_tok], values[half_tok:])
+        return first_half.astype(jnp.bfloat16), second_half.astype(jnp.bfloat16)
+
+    def pack_filter(block):
+        return packed(filt[:, columns(block)].astype(jnp.float32))
+
+    def send_filter(to):
+        filt_out[0, to], filt_out[1, to] = pack_filter(to)
+        filter_copy(0, to, me).start()
+
+    each_partner(send_filter)
+    filt_in[0, me], filt_in[1, me] = pack_filter(me)
 
     load.wait()
 
@@ -213,106 +239,136 @@
         taps = taps_ref[:, cols].astype(jnp.float32)
         rows = jnp.concatenate(
             [halo[:, cols].astype(jnp.float32), proj[:, cols].astype(jnp.float32)], 0)
-        count = taps.shape[0]
         total = None
-        for tap in range(count):
+        for tap in range(taps.shape[0]):
             start = ROWS - tap
             term = taps[tap:tap + 1] * rows[start:start + tok]
             total = term if total is None else total + term
         return total
 
-    def gate(block):
-        return (featured(block, 1) * featured(block, 2)).astype(jnp.bfloat16)
+    def make_gate(block):
+        rounded = (featured(block, 1) * featured(block, 2)).astype(jnp.bfloat16)
+        gated[block] = rounded
+        return packed(rounded.astype(jnp.float32))
 
     def send_gate(to):
-        gate_out[to] = gate(to)
-        gate_copy(to, me, me).start()
+        gate_out[0, to], gate_out[1, to] = make_gate(to)
+        gate_copy(0, to, me).start()
 
     each_partner(send_gate)
-    own_gate = gate(me)
-    gate_out[me] = own_gate
-    gate_in[me] = own_gate
-
+    gate_in[0, me], gate_in[1, me] = make_gate(me)
+
+    left = lax.broadcasted_iota(jnp.int32, (half_tok, LANES), 1) < HALF
     for freq in range(freqs):
         for part in range(2):
-            turn[freq, part] = jnp.broadcast_to(
-                turn_ref[part][:, freq:freq + 1], (tok, LANES))
-
-    def ask(block, carry):
-        query[block] = featured(block, 0)
-        return carry
-
-    lax.fori_loop(0, n, ask, 0)
-
-    def first_section(source):
-        def run(tile, carry):
-            rows = pl.ds(pl.multiple_of(tile * ROWS, ROWS), ROWS)
-            low = pl.ds(pl.multiple_of(tok + tile * ROWS, ROWS), ROWS)
-            spec = forward64([source[b, rows, :].astype(jnp.float32) for b in range(n)])
-            for freq in range(freqs):
+            column = turn_ref[part][:, freq:freq + 1]
+            turn[freq, part] = jnp.where(left, column[:half_tok], column[half_tok:])
+    first[quads - 1] = jnp.zeros(first.shape[1:], first.dtype)
+
+    def spot(tile, shift):
+        return pl.ds(pl.multiple_of(shift + tile * ROWS, ROWS), ROWS)
+
+    def pair_lanes(pair):
+        return pair // 2, slice((pair % 2) * LANES, (pair % 2 + 1) * LANES)
+
+    def first_section(source, half):
+        def run(tile):
+            rows = spot(tile, 0)
+            spec = forward64([source[half, b, rows, :].astype(jnp.float32) for b in range(n)])
+
+            def turned(freq):
                 cos, sin = turn[freq, 0, rows, :], turn[freq, 1, rows, :]
                 z = spec[freq]
                 if z.im is None:
-                    re, im = z.re * cos, -(z.re * sin)
-                else:
-                    re, im = z.re * cos + z.im * sin, z.im * cos - z.re * sin
-                first[freq, rows, :] = re.astype(jnp.bfloat16)
-                first[freq, low, :] = im.astype(jnp.bfloat16)
-            return carry
-        lax.fori_loop(0, tok // ROWS, run, 0)
-
-    own.wait()
-    each_partner(lambda src: filter_copy(src, src, src).wait_recv())
-    first_section(filt_in)
-
-    def filter_spectrum(freq, carry):
-        fspec[freq] = jnp.dot(fwd_ref[...], first[freq], preferred_element_type=jnp.float32)
-        return carry
-
-    lax.fori_loop(0, freqs, filter_spectrum, 0)
-
-    each_partner(lambda src: gate_copy(src, src, src).wait_recv())
-    first_section(gate_in)
-
-    def through(freq, carry):
-        spec = jnp.dot(fwd_ref[...], first[freq], preferred_element_type=jnp.float32)
-        sr, si = spec[:tok], spec[tok:]
-        fr, fi = fspec[freq, :tok], fspec[freq, tok:]
-        product = jnp.concatenate([sr * fr - si * fi, sr * fi + si * fr], 0).astype(jnp.bfloat16)
-        result = jnp.dot(bwd_ref[...], product, preferred_element_type=jnp.float32)
-        br, bi = result[:tok], result[tok:]
-        cos, sin = turn[freq, 0], turn[freq, 1]
-        back[freq, :tok] = br * cos - bi * sin
-        back[freq, tok:] = bi * cos + br * sin
-        return carry
-
-    lax.fori_loop(0, freqs, through, 0)
+                    return z.re * cos, -(z.re * sin)
+                return z.re * cos + z.im * sin, z.im * cos - z.re * sin
+
+            for pair in range((freqs + 1) // 2):
+                even = turned(2 * pair)
+                odd = turned(2 * pair + 1) if 2 * pair + 1 < freqs else even
+                quad, lanes = pair_lanes(pair)
+                for part in range(2):
+                    low, high = swapped_halves(even[part], odd[part])
+                    first[quad, spot(tile, part * tok), lanes] = low.astype(jnp.bfloat16)
+                    first[quad, spot(tile, part * tok + half_tok), lanes] = high.astype(jnp.bfloat16)
+        loop(half_tok // ROWS, run)
+
+    def spectrum(quad):
+        return jnp.dot(fwd_ref[...], first[quad], preferred_element_type=jnp.float32)
+
+    def filter_section(half):
+        first_section(filt_in, half)
+        for quad in range(quads):
+            fspec[quad] = spectrum(quad)
+
+    def signal_section(half):
+        first_section(gate_in, half)
+        for quad in range(quads):
+            spec = spectrum(quad)
+            sr, si = spec[:tok], spec[tok:]
+            fr, fi = fspec[quad, :tok], fspec[quad, tok:]
+            product = jnp.concatenate([sr * fr - si * fi, sr * fi + si * fr], 0).astype(jnp.bfloat16)
+            back[quad] = jnp.dot(bwd_ref[...], product, preferred_element_type=jnp.float32)
 
     scale = 1.0 / (2 * n * tok)
 
-    def last_section(tile, carry):
-        rows = pl.ds(pl.multiple_of(tile * ROWS, ROWS), ROWS)
-        low = pl.ds(pl.multiple_of(tok + tile * ROWS, ROWS), ROWS)
-        done = backward64([Cx(back[freq, rows, :], back[freq, low, :]) for freq in range(freqs)])
-        for b in range(n):
-            conv_out[b, rows, :] = (done[b] * scale).astype(jnp.bfloat16)
-        return carry
-
-    lax.fori_loop(0, tok // ROWS, last_section, 0)
-
-    each_partner(lambda to: conv_copy(to, me, me).start())
-
-    def finish(block, rows):
+    def last_section(half):
+        def run(tile):
+            rows = spot(tile, 0)
+            spec = []
+            for pair in range((freqs + 1) // 2):
+                quad, lanes = pair_lanes(pair)
+                parts = [
+                    swapped_halves(
+                        back[quad, spot(tile, part * tok), lanes],
+                        back[quad, spot(tile, part * tok + half_tok), lanes])
+                    for part in range(2)
+                ]
+                for odd in range(2):
+                    freq = 2 * pair + odd
+                    if freq < freqs:
+                        re, im = parts[0][odd], parts[1][odd]
+                        cos, sin = turn[freq, 0, rows, :], turn[freq, 1, rows, :]
+                        spec.append(Cx(re * cos - im * sin, im * cos + re * sin))
+            done = backward64(spec)
+            for b in range(n):
+                conv_out[half, b, rows, :] = (done[b] * scale).astype(jnp.bfloat16)
+        loop(half_tok // ROWS, run)
+
+    receive_all(filter_copy, 0)
+    send_all(filter_copy, 1)
+    filter_section(0)
+    receive_all(gate_copy, 0)
+    send_all(gate_copy, 1)
+    signal_section(0)
+    last_section(0)
+    send_all(conv_copy, 0)
+
+    def ask(block):
+        query[block] = featured(block, 0)
+
+    loop(n, ask)
+
+    receive_all(filter_copy, 1)
+    filter_section(1)
+    receive_all(gate_copy, 1)
+    signal_section(1)
+    last_section(1)
+    send_all(conv_copy, 1)
+
+    def finish(block, source):
         cols = columns(block)
-        mixed = query[block] * (
-            rows.astype(jnp.float32) + skip_ref[:, cols] * gate_out[block].astype(jnp.float32))
+        rows = jnp.concatenate(swapped_halves(
+            source[0, block].astype(jnp.float32), source[1, block].astype(jnp.float32)), 0)
+        mixed = query[block] * (rows + skip_ref[:, cols] * gated[block].astype(jnp.float32))
         out_ref[:, cols] = mixed.astype(jnp.bfloat16)
 
-    finish(me, conv_out[me])
+    finish(me, conv_out)
 
     def take(src):
-        conv_copy(src, src, src).wait_recv()
-        finish(src, conv_in[src])
+        conv_copy(0, src, src).wait_recv()
+        conv_copy(1, src, src).wait_recv()
+        finish(src, conv_in)
 
     each_partner(take)
 
@@ -321,9 +377,10 @@
         halo_copy(me + 1).wait_send()
 
     def sent(to):
-        filter_copy(to, me, me).wait_send()
-        gate_copy(to, me, me).wait_send()
-        conv_copy(to, me, me).wait_send()
+        for half in range(2):
+            filter_copy(half, to, me).wait_send()
+            gate_copy(half, to, me).wait_send()
+            conv_copy(half, to, me).wait_send()
 
     each_partner(sent)
 
@@ -344,7 +401,8 @@
     turns = np.stack(cosines(tok, LANES, 2 * n * tok)).astype(np.float32)
     vmem = pl.BlockSpec(memory_space=pltpu.VMEM)
     hbm = pl.BlockSpec(memory_space=pl.ANY)
-    block = (n, tok, LANES)
+    quads = -(-freqs // 4)
+    chunks = pltpu.VMEM((2, n, tok // 2, LANES), jnp.bfloat16)
     dma = pltpu.SemaphoreType.DMA
     return pl.pallas_call(
         functools.partial(kernel, n, n_inner),
@@ -353,19 +411,17 @@
         out_specs=vmem,
         scratch_shapes=[
             pltpu.VMEM(projected.shape, jnp.bfloat16),
+            pltpu.VMEM(long_filter.shape, jnp.bfloat16),
             pltpu.VMEM((ROWS, projected.shape[1]), jnp.bfloat16),
-            pltpu.VMEM(block, jnp.bfloat16),
-            pltpu.VMEM(block, jnp.bfloat16),
-            pltpu.VMEM(block, jnp.bfloat16),
-            pltpu.VMEM(block, jnp.bfloat16),
-            pltpu.VMEM(block, jnp.bfloat16),
-            pltpu.VMEM((freqs, 2 * tok, LANES), jnp.bfloat16),
-            pltpu.VMEM((freqs, 2 * tok, LANES), jnp.float32),
-            pltpu.VMEM((freqs, 2 * tok, LANES), jnp.float32),
-            pltpu.VMEM((freqs, 2, tok, LANES), jnp.float32),
-            pltpu.VMEM(block, jnp.float32),
+            chunks, chunks, chunks, chunks, chunks, chunks,
+            pltpu.VMEM((n, tok, LANES), jnp.bfloat16),
+            pltpu.VMEM((quads, 2 * tok, 4 * HALF), jnp.bfloat16),
+            pltpu.VMEM((quads, 2 * tok, 4 * HALF), jnp.float32),
+            pltpu.VMEM((quads, 2 * tok, 4 * HALF), jnp.float32),
+            pltpu.VMEM((freqs, 2, tok // 2, LANES), jnp.float32),
+            pltpu.VMEM((n, tok, LANES), jnp.float32),
             dma, dma, dma, dma,
-            dma((n,)), dma((n,)), dma((n,)), dma((n,)), dma((n,)), dma((n,)),
+            dma((2, n)), dma((2, n)), dma((2, n)), dma((2, n)), dma((2, n)), dma((2, n)),
         ],
         compiler_params=pltpu.CompilerParams(
             collective_id=0, has_side_effects=True, vmem_limit_bytes=56 * 1024 * 1024),

time: 109 us -> 97.9 us (0.90)
  Pallas kernels: 107 us -> 95.4 us
    pallas_call x1, Pallas kernels: 107 us -> 95.4 us  [by_channels(): pl.pallas_call(functools.partial(kernel, n, n_inner), out_shape=jax.Shape...]
where the time goes in v1:
time: 97.9 us; the launch traced here: 97.7 us
  Pallas kernels  95.4 us (97%)
  local copies, waits for them, and re-layouts  2.29 us (2%)
    pallas_call x1, Pallas kernels, by_channels(): pl.pallas_call(functools.partial(kernel, n, n_inner), out_shape=jax.Shape...  95.4 us
    unnamed x1, local copies, waits for them, and re-layouts  2.29 us

profile of v1, /device:TPU:1, one launch (start us, length us, event | category | flops | bytes accessed | tf_op | source)
XLA Modules:
  0.0 97.7 jit_solution(1596224778533198100)
XLA Ops:
  0.0 95.4 %shard_map.73 = bf16[128,4096]{1,0:T(8,128)(2,1)} custom-call(bf16[128,12288]{1,0:T(8,128)(2,1)} %proj_hbm.1, bf16[128,4096]{1,0:T(8,128)(2,1)} %filt_hbm.1, bf16[3,12288]{1,0:T(4,128)(2,1)} %taps_ref.1, f32[1,4096]{1,0:T(1,128)} %bitcast.1, bf16[256,256]{1,0:T(8,128)(2,1)} %constant.6.clone.fwd_ref, bf16[256,256]{1,0:T(8,128)(2,1)} %constant.7.clone.bwd_ref, ...), custom_call_target="tpu_custom_call" | custom-call | flops 1660944384 | bytes 5242880 | tf_op jit(solution)/shard_map/pallas_call | solution.py:407
  95.4 2.3 %copy.9 = bf16[128,4096]{1,0:T(8,128)(2,1)} copy(bf16[128,4096]{1,0:T(8,128)(2,1)} %shard_map.73) | data formatting | bytes 2097152

commit v2 on v1

--- a/solution.py
+++ b/solution.py
@@ -160,11 +160,27 @@
     def columns(block, part=0):
         return pl.ds(pl.multiple_of(part * width + block * LANES, LANES), LANES)
 
+    n_z, n_outer = n_inner // 2, n // n_inner
+    n_x = n_outer // 2
+    x, core, z, y = outer // 2, outer % 2, inner // 2, inner % 2
+
+    def partner(step):
+        turn_of = step // n_z
+        to_z = (z + step + (n_z // 2) * core) % n_z
+        to_x = (x + turn_of + y) % n_x
+        to_y = (y + turn_of // n_x + core) % 2
+        to_core = (core + turn_of // (2 * n_x)) % 2
+        return (to_x * 2 + to_core) * n_inner + to_z * 2 + to_y
+
     def each_partner(body):
         def run(step, carry):
-            body(lax.rem(me + step, n))
+            to = partner(step)
+
+            @pl.when(to != me)
+            def _():
+                body(to)
             return carry
-        lax.fori_loop(1, n, run, 0)
+        lax.fori_loop(0, n, run, 0)
 
     def loop(count, body):
         def run(step, carry):

time: 97.9 us -> 96.3 us (0.984)
  Pallas kernels: 95.4 us -> 93 us
    pallas_call x1, Pallas kernels: 95.4 us -> 93 us  [by_channels(): pl.pallas_call(functools.partial(kernel, n, n_inner), out_shape=jax.Shape...]
where the time goes in v2:
time: 96.3 us; the launch traced here: 95.2 us
  Pallas kernels  93 us (97%)
  local copies, waits for them, and re-layouts  2.29 us (2%)
    pallas_call x1, Pallas kernels, by_channels(): pl.pallas_call(functools.partial(kernel, n, n_inner), out_shape=jax.Shape...  93 us
    unnamed x1, local copies, waits for them, and re-layouts  2.29 us

profile of v2, /device:TPU:1, one launch (start us, length us, event | category | flops | bytes accessed | tf_op | source)
XLA Modules:
  0.0 95.2 jit_solution(16913582738202691243)
XLA Ops:
  0.0 93.0 %shard_map.73 = bf16[128,4096]{1,0:T(8,128)(2,1)} custom-call(bf16[128,12288]{1,0:T(8,128)(2,1)} %proj_hbm.1, bf16[128,4096]{1,0:T(8,128)(2,1)} %filt_hbm.1, bf16[3,12288]{1,0:T(4,128)(2,1)} %taps_ref.1, f32[1,4096]{1,0:T(1,128)} %bitcast.1, bf16[256,256]{1,0:T(8,128)(2,1)} %constant.6.clone.fwd_ref, bf16[256,256]{1,0:T(8,128)(2,1)} %constant.7.clone.bwd_ref, ...), custom_call_target="tpu_custom_call" | custom-call | flops 1660944384 | bytes 5242880 | tf_op jit(solution)/shard_map/pallas_call | solution.py:423
  93.0 2.3 %copy.9 = bf16[128,4096]{1,0:T(8,128)(2,1)} copy(bf16[128,4096]{1,0:T(8,128)(2,1)} %shard_map.73) | data formatting | bytes 2097152

commit v3 on v1

--- a/solution.py
+++ b/solution.py
@@ -14,6 +14,7 @@
 LANES = 128
 HALF = LANES // 2
 ROWS = 16
+SUB = 8
 RADIX = 8
 
 
@@ -143,9 +144,9 @@
 
 def kernel(
     n, n_inner, proj_hbm, filt_hbm, taps_ref, skip_ref, fwd_ref, bwd_ref, turn_ref, out_ref,
-    proj, filt, halo, filt_out, gate_out, conv_out, filt_in, gate_in, conv_in,
+    proj, filt, halo, halo_out, halo_in, filt_out, gate_out, conv_out, filt_in, gate_in, conv_in,
     gated, first, fspec, back, turn, query,
-    proj_sem, filt_sem, halo_send, halo_recv, f_send, f_recv, g_send, g_recv, y_send, y_recv,
+    proj_sem, filt_sem, halo_send, halo_recv, f_sems, g_sems, y_sems,
 ):
     tok, width = filt.shape
     freqs = n + 1
@@ -154,17 +155,32 @@
     outer, inner = lax.axis_index("outer"), lax.axis_index("inner")
     me = outer * n_inner + inner
 
-    def place(device):
-        return (device // n_inner, device % n_inner)
-
     def columns(block, part=0):
         return pl.ds(pl.multiple_of(part * width + block * LANES, LANES), LANES)
 
+    n_z = n_inner // 2
+    n_x = n // n_inner // 2
+    x, core = lax.div(outer, 2), lax.rem(outer, 2)
+    z, y = lax.div(inner, 2), lax.rem(inner, 2)
+
+    def partner(step):
+        turn_of = lax.div(step, n_z)
+        to_z = lax.rem(z + step + (n_z // 2) * core, n_z)
+        to_x = lax.rem(x + turn_of + y, n_x)
+        to_y = lax.rem(y + lax.div(turn_of, n_x) + core, 2)
+        to_core = lax.rem(core + lax.div(turn_of, 2 * n_x), 2)
+        to = (to_x * 2 + to_core, to_z * 2 + to_y)
+        return to, to[0] * n_inner + to[1]
+
     def each_partner(body):
         def run(step, carry):
-            body(lax.rem(me + step, n))
+            to, number = partner(step)
+
+            @pl.when(number != me)
+            def _():
+                body(to, number)
             return carry
-        lax.fori_loop(1, n, run, 0)
+        lax.fori_loop(0, n, run, 0)
 
     def loop(count, body):
         def run(step, carry):
@@ -174,35 +190,41 @@
 
     def halo_copy(to):
         return pltpu.make_async_remote_copy(
-            src_ref=proj_hbm.at[pl.ds(tok - ROWS, ROWS), :], dst_ref=halo,
-            send_sem=halo_send, recv_sem=halo_recv, device_id=place(to), device_id_type=MESH,
+            src_ref=halo_out, dst_ref=halo_in, send_sem=halo_send, recv_sem=halo_recv,
+            device_id=(lax.div(to, n_inner), lax.rem(to, n_inner)), device_id_type=MESH,
         )
 
-    def chunk_copy(source, target, send, recv, half, to, slot):
-        return pltpu.make_async_remote_copy(
-            src_ref=source.at[half, to], dst_ref=target.at[half, slot],
-            send_sem=send.at[half, to], recv_sem=recv.at[half, slot],
-            device_id=place(to), device_id_type=MESH,
-        )
-
-    filter_copy = functools.partial(chunk_copy, filt_out, filt_in, f_send, f_recv)
-    gate_copy = functools.partial(chunk_copy, gate_out, gate_in, g_send, g_recv)
-    conv_copy = functools.partial(chunk_copy, conv_out, conv_in, y_send, y_recv)
-
-    def send_all(copy, half):
-        each_partner(lambda to: copy(half, to, me).start())
-
-    def receive_all(copy, half):
-        each_partner(lambda src: copy(half, src, src).wait_recv())
-
+    def send(source, target, sems, half, to, number):
+        pltpu.make_async_remote_copy(
+            src_ref=source.at[half, number], dst_ref=target.at[half, me],
+            send_sem=sems.at[0, half], recv_sem=sems.at[1, half],
+            device_id=to, device_id_type=MESH,
+        ).start()
+
+    def wait_all(buffer, sems, way, half):
+        chunks = buffer.at[half, pl.ds(0, n - 1)]
+        pltpu.make_async_copy(chunks, chunks, sems.at[way, half]).wait()
+
+    send_filter = functools.partial(send, filt_out, filt_in, f_sems)
+    send_gate = functools.partial(send, gate_out, gate_in, g_sems)
+    send_conv = functools.partial(send, conv_out, conv_in, y_sems)
+
+    load = pltpu.make_async_copy(proj_hbm, proj, proj_sem)
+    load.start()
     load_filt = pltpu.make_async_copy(filt_hbm, filt, filt_sem)
     load_filt.start()
-    load = pltpu.make_async_copy(proj_hbm, proj, proj_sem)
-    load.start()
 
     barrier = pltpu.get_barrier_semaphore()
-    each_partner(lambda to: pl.semaphore_signal(
-        barrier, inc=1, device_id=place(to), device_id_type=MESH))
+    each_partner(lambda to, number: pl.semaphore_signal(
+        barrier, inc=1, device_id=to, device_id_type=MESH))
+
+    load.wait()
+    blocks = proj.shape[1] // LANES
+    for block in range(blocks):
+        tail = proj[tok - ROWS:, block * LANES:(block + 1) * LANES].astype(jnp.float32)
+        halo[2 * block:2 * block + 2, :] = tail[ROWS - 2:]
+    halo_out[...] = halo[...].astype(jnp.bfloat16)
+
     load_filt.wait()
     pl.semaphore_wait(barrier, n - 1)
 
@@ -217,14 +239,12 @@
     def pack_filter(block):
         return packed(filt[:, columns(block)].astype(jnp.float32))
 
-    def send_filter(to):
-        filt_out[0, to], filt_out[1, to] = pack_filter(to)
-        filter_copy(0, to, me).start()
-
-    each_partner(send_filter)
+    def start_filter(to, number):
+        filt_out[0, number], filt_out[1, number] = pack_filter(number)
+        send_filter(0, to, number)
+
+    each_partner(start_filter)
     filt_in[0, me], filt_in[1, me] = pack_filter(me)
-
-    load.wait()
 
     @pl.when(me == 0)
     def _():
@@ -233,15 +253,19 @@
     @pl.when(me > 0)
     def _():
         halo_copy(me).wait_recv()
+        halo[...] = halo_in[...].astype(jnp.float32)
+
+    upper = lax.broadcasted_iota(jnp.int32, (SUB, LANES), 0) < SUB - 1
 
     def featured(block, part):
         cols = columns(block, part)
         taps = taps_ref[:, cols].astype(jnp.float32)
-        rows = jnp.concatenate(
-            [halo[:, cols].astype(jnp.float32), proj[:, cols].astype(jnp.float32)], 0)
+        at = 2 * (part * (width // LANES) + block)
+        head = jnp.where(upper, halo[pl.ds(at, 1), :], halo[pl.ds(at + 1, 1), :])
+        rows = jnp.concatenate([head, proj[:, cols].astype(jnp.float32)], 0)
         total = None
         for tap in range(taps.shape[0]):
-            start = ROWS - tap
+            start = SUB - tap
             term = taps[tap:tap + 1] * rows[start:start + tok]
             total = term if total is None else total + term
         return total
@@ -251,12 +275,13 @@
         gated[block] = rounded
         return packed(rounded.astype(jnp.float32))
 
-    def send_gate(to):
-        gate_out[0, to], gate_out[1, to] = make_gate(to)
-        gate_copy(0, to, me).start()
-
-    each_partner(send_gate)
+    def start_gate(to, number):
+        gate_out[0, number], gate_out[1, number] = make_gate(number)
+        send_gate(0, to, number)
+
+    each_partner(start_gate)
     gate_in[0, me], gate_in[1, me] = make_gate(me)
+    each_partner(lambda to, number: send_filter(1, to, number))
 
     left = lax.broadcasted_iota(jnp.int32, (half_tok, LANES), 1) < HALF
     for freq in range(freqs):
@@ -335,54 +360,47 @@
                 conv_out[half, b, rows, :] = (done[b] * scale).astype(jnp.bfloat16)
         loop(half_tok // ROWS, run)
 
-    receive_all(filter_copy, 0)
-    send_all(filter_copy, 1)
+    wait_all(filt_in, f_sems, 1, 0)
+    each_partner(lambda to, number: send_gate(1, to, number))
     filter_section(0)
-    receive_all(gate_copy, 0)
-    send_all(gate_copy, 1)
+    wait_all(gate_in, g_sems, 1, 0)
     signal_section(0)
     last_section(0)
-    send_all(conv_copy, 0)
+    each_partner(lambda to, number: send_conv(0, to, number))
 
     def ask(block):
         query[block] = featured(block, 0)
 
     loop(n, ask)
 
-    receive_all(filter_copy, 1)
+    wait_all(filt_in, f_sems, 1, 1)
     filter_section(1)
-    receive_all(gate_copy, 1)
+    wait_all(gate_in, g_sems, 1, 1)
     signal_section(1)
     last_section(1)
-    send_all(conv_copy, 1)
-
-    def finish(block, source):
+    each_partner(lambda to, number: send_conv(1, to, number))
+
+    for half in range(2):
+        conv_in[half, me] = conv_out[half, me]
+        wait_all(conv_in, y_sems, 1, half)
+
+    def finish(block):
         cols = columns(block)
         rows = jnp.concatenate(swapped_halves(
-            source[0, block].astype(jnp.float32), source[1, block].astype(jnp.float32)), 0)
+            conv_in[0, block].astype(jnp.float32), conv_in[1, block].astype(jnp.float32)), 0)
         mixed = query[block] * (rows + skip_ref[:, cols] * gated[block].astype(jnp.float32))
         out_ref[:, cols] = mixed.astype(jnp.bfloat16)
 
-    finish(me, conv_out)
-
-    def take(src):
-        conv_copy(0, src, src).wait_recv()
-        conv_copy(1, src, src).wait_recv()
-        finish(src, conv_in)
-
-    each_partner(take)
+    loop(n, finish)
 
     @pl.when(me < n - 1)
     def _():
         halo_copy(me + 1).wait_send()
 
-    def sent(to):
-        for half in range(2):
-            filter_copy(half, to, me).wait_send()
-            gate_copy(half, to, me).wait_send()
-            conv_copy(half, to, me).wait_send()
-
-    each_partner(sent)
+    for half in range(2):
+        wait_all(filt_out, f_sems, 0, half)
+        wait_all(gate_out, g_sems, 0, half)
+        wait_all(conv_out, y_sems, 0, half)
 
 
 def cosines(rows, cols, length):
@@ -402,6 +420,7 @@
     vmem = pl.BlockSpec(memory_space=pltpu.VMEM)
     hbm = pl.BlockSpec(memory_space=pl.ANY)
     quads = -(-freqs // 4)
+    edges = 2 * projected.shape[1] // LANES
     chunks = pltpu.VMEM((2, n, tok // 2, LANES), jnp.bfloat16)
     dma = pltpu.SemaphoreType.DMA
     return pl.pallas_call(
@@ -412,7 +431,9 @@
         scratch_shapes=[
             pltpu.VMEM(projected.shape, jnp.bfloat16),
             pltpu.VMEM(long_filter.shape, jnp.bfloat16),
-            pltpu.VMEM((ROWS, projected.shape[1]), jnp.bfloat16),
+            pltpu.VMEM((edges, LANES), jnp.float32),
+            pltpu.VMEM((edges, LANES), jnp.bfloat16),
+            pltpu.VMEM((edges, LANES), jnp.bfloat16),
             chunks, chunks, chunks, chunks, chunks, chunks,
             pltpu.VMEM((n, tok, LANES), jnp.bfloat16),
             pltpu.VMEM((quads, 2 * tok, 4 * HALF), jnp.bfloat16),
@@ -421,7 +442,7 @@
             pltpu.VMEM((freqs, 2, tok // 2, LANES), jnp.float32),
             pltpu.VMEM((n, tok, LANES), jnp.float32),
             dma, dma, dma, dma,
-            dma((2, n)), dma((2, n)), dma((2, n)), dma((2, n)), dma((2, n)), dma((2, n)),
+            dma((2, 2)), dma((2, 2)), dma((2, 2)),
         ],
         compiler_params=pltpu.CompilerParams(
             collective_id=0, has_side_effects=True, vmem_limit_bytes=56 * 1024 * 1024),

time: 97.9 us -> 84.3 us (0.86)
  Pallas kernels: 95.4 us -> 81.9 us
    pallas_call x1, Pallas kernels: 95.4 us -> 81.9 us  [by_channels(): pl.pallas_call(functools.partial(kernel, n, n_inner), out_shape=jax.Shape...]
where the time goes in v3:
time: 84.3 us; the launch traced here: 84.2 us
  Pallas kernels  81.9 us (97%)
  local copies, waits for them, and re-layouts  2.29 us (3%)
    pallas_call x1, Pallas kernels, by_channels(): pl.pallas_call(functools.partial(kernel, n, n_inner), out_shape=jax.Shape...  81.9 us
    unnamed x1, local copies, waits for them, and re-layouts  2.29 us

profile of v3, /device:TPU:1, one launch (start us, length us, event | category | flops | bytes accessed | tf_op | source)
XLA Modules:
  0.0 84.2 jit_solution(15317225529840740577)
XLA Ops:
  0.0 81.9 %shard_map.73 = bf16[128,4096]{1,0:T(8,128)(2,1)} custom-call(bf16[128,12288]{1,0:T(8,128)(2,1)} %proj_hbm.1, bf16[128,4096]{1,0:T(8,128)(2,1)} %filt_hbm.1, bf16[3,12288]{1,0:T(4,128)(2,1)} %taps_ref.1, f32[1,4096]{1,0:T(1,128)} %bitcast.1, bf16[256,256]{1,0:T(8,128)(2,1)} %constant.6.clone.fwd_ref, bf16[256,256]{1,0:T(8,128)(2,1)} %constant.7.clone.bwd_ref, ...), custom_call_target="tpu_custom_call" | custom-call | flops 1660944384 | bytes 5242880 | tf_op jit(solution)/shard_map/pallas_call | solution.py:426
  81.9 2.3 %copy.9 = bf16[128,4096]{1,0:T(8,128)(2,1)} copy(bf16[128,4096]{1,0:T(8,128)(2,1)} %shard_map.73) | data formatting | bytes 2097152

commit v4 on v3

--- a/solution.py
+++ b/solution.py
@@ -145,8 +145,8 @@
 def kernel(
     n, n_inner, proj_hbm, filt_hbm, taps_ref, skip_ref, fwd_ref, bwd_ref, turn_ref, out_ref,
     proj, filt, halo, halo_out, halo_in, filt_out, gate_out, conv_out, filt_in, gate_in, conv_in,
-    gated, first, fspec, back, turn, query,
-    proj_sem, filt_sem, halo_send, halo_recv, f_sems, g_sems, y_sems,
+    gated, first, fspec, back, turn, query, direct, tail,
+    tail_sem, proj_sem, filt_sem, halo_send, halo_recv, f_sems, g_sems, y_sems,
 ):
     tok, width = filt.shape
     freqs = n + 1
@@ -209,20 +209,23 @@
     send_gate = functools.partial(send, gate_out, gate_in, g_sems)
     send_conv = functools.partial(send, conv_out, conv_in, y_sems)
 
+    load_tail = pltpu.make_async_copy(
+        proj_hbm.at[pl.ds(tok - ROWS, ROWS), :], tail, tail_sem)
+    load_tail.start()
+    load_filt = pltpu.make_async_copy(filt_hbm, filt, filt_sem)
+    load_filt.start()
     load = pltpu.make_async_copy(proj_hbm, proj, proj_sem)
     load.start()
-    load_filt = pltpu.make_async_copy(filt_hbm, filt, filt_sem)
-    load_filt.start()
 
     barrier = pltpu.get_barrier_semaphore()
     each_partner(lambda to, number: pl.semaphore_signal(
         barrier, inc=1, device_id=to, device_id_type=MESH))
 
-    load.wait()
+    load_tail.wait()
     blocks = proj.shape[1] // LANES
     for block in range(blocks):
-        tail = proj[tok - ROWS:, block * LANES:(block + 1) * LANES].astype(jnp.float32)
-        halo[2 * block:2 * block + 2, :] = tail[ROWS - 2:]
+        last = tail[:, block * LANES:(block + 1) * LANES].astype(jnp.float32)
+        halo[2 * block:2 * block + 2, :] = last[ROWS - 2:]
     halo_out[...] = halo[...].astype(jnp.bfloat16)
 
     load_filt.wait()
@@ -245,6 +248,8 @@
 
     each_partner(start_filter)
     filt_in[0, me], filt_in[1, me] = pack_filter(me)
+
+    load.wait()
 
     @pl.when(me == 0)
     def _():
@@ -366,19 +371,20 @@
     wait_all(gate_in, g_sems, 1, 0)
     signal_section(0)
     last_section(0)
-    each_partner(lambda to, number: send_conv(0, to, number))
-
-    def ask(block):
-        query[block] = featured(block, 0)
-
-    loop(n, ask)
-
     wait_all(filt_in, f_sems, 1, 1)
     filter_section(1)
     wait_all(gate_in, g_sems, 1, 1)
+    each_partner(lambda to, number: send_conv(0, to, number))
     signal_section(1)
     last_section(1)
     each_partner(lambda to, number: send_conv(1, to, number))
+
+    def ask(block):
+        asked = featured(block, 0)
+        query[block] = asked
+        direct[block] = asked * (skip_ref[:, columns(block)] * gated[block].astype(jnp.float32))
+
+    loop(n, ask)
 
     for half in range(2):
         conv_in[half, me] = conv_out[half, me]
@@ -388,8 +394,7 @@
         cols = columns(block)
         rows = jnp.concatenate(swapped_halves(
             conv_in[0, block].astype(jnp.float32), conv_in[1, block].astype(jnp.float32)), 0)
-        mixed = query[block] * (rows + skip_ref[:, cols] * gated[block].astype(jnp.float32))
-        out_ref[:, cols] = mixed.astype(jnp.bfloat16)
+        out_ref[:, cols] = (query[block] * rows + direct[block]).astype(jnp.bfloat16)
 
     loop(n, finish)
 
@@ -441,7 +446,9 @@
             pltpu.VMEM((quads, 2 * tok, 4 * HALF), jnp.float32),
             pltpu.VMEM((freqs, 2, tok // 2, LANES), jnp.float32),
             pltpu.VMEM((n, tok, LANES), jnp.float32),
-            dma, dma, dma, dma,
+            pltpu.VMEM((n, tok, LANES), jnp.float32),
+            pltpu.VMEM((ROWS, projected.shape[1]), jnp.bfloat16),
+            dma, dma, dma, dma, dma,
             dma((2, 2)), dma((2, 2)), dma((2, 2)),
         ],
         compiler_params=pltpu.CompilerParams(

time: 84.3 us -> 86.1 us (1.021)
  Pallas kernels: 81.9 us -> 83.6 us
    pallas_call x1, Pallas kernels: 81.9 us -> 83.6 us  [by_channels(): pl.pallas_call(functools.partial(kernel, n, n_inner), out_shape=jax.Shape...]
where the time goes in v4:
time: 86.1 us; the launch traced here: 85.9 us
  Pallas kernels  83.6 us (97%)
  local copies, waits for them, and re-layouts  2.29 us (3%)
    pallas_call x1, Pallas kernels, by_channels(): pl.pallas_call(functools.partial(kernel, n, n_inner), out_shape=jax.Shape...  83.6 us
    unnamed x1, local copies, waits for them, and re-layouts  2.29 us

profile of v4, /device:TPU:1, one launch (start us, length us, event | category | flops | bytes accessed | tf_op | source)
XLA Modules:
  0.0 85.9 jit_solution(15752134943186164465)
XLA Ops:
  0.0 83.6 %shard_map.73 = bf16[128,4096]{1,0:T(8,128)(2,1)} custom-call(bf16[128,12288]{1,0:T(8,128)(2,1)} %proj_hbm.1, bf16[128,4096]{1,0:T(8,128)(2,1)} %filt_hbm.1, bf16[3,12288]{1,0:T(4,128)(2,1)} %taps_ref.1, f32[1,4096]{1,0:T(1,128)} %bitcast.1, bf16[256,256]{1,0:T(8,128)(2,1)} %constant.6.clone.fwd_ref, bf16[256,256]{1,0:T(8,128)(2,1)} %constant.7.clone.bwd_ref, ...), custom_call_target="tpu_custom_call" | custom-call | flops 1660944384 | bytes 5242880 | tf_op jit(solution)/shard_map/pallas_call | solution.py:431
  83.6 2.3 %copy.9 = bf16[128,4096]{1,0:T(8,128)(2,1)} copy(bf16[128,4096]{1,0:T(8,128)(2,1)} %shard_map.73) | data formatting | bytes 2097152

commit v5 on v4

--- a/solution.py
+++ b/solution.py
@@ -371,10 +371,10 @@
     wait_all(gate_in, g_sems, 1, 0)
     signal_section(0)
     last_section(0)
+    each_partner(lambda to, number: send_conv(0, to, number))
     wait_all(filt_in, f_sems, 1, 1)
     filter_section(1)
     wait_all(gate_in, g_sems, 1, 1)
-    each_partner(lambda to, number: send_conv(0, to, number))
     signal_section(1)
     last_section(1)
     each_partner(lambda to, number: send_conv(1, to, number))

time: 86.1 us -> 84.3 us (0.979)
  Pallas kernels: 83.6 us -> 81.8 us
    pallas_call x1, Pallas kernels: 83.6 us -> 81.8 us  [by_channels(): pl.pallas_call(functools.partial(kernel, n, n_inner), out_shape=jax.Shape...]
where the time goes in v5:
time: 84.3 us; the launch traced here: 84.1 us
  Pallas kernels  81.8 us (97%)
  local copies, waits for them, and re-layouts  2.29 us (3%)
    pallas_call x1, Pallas kernels, by_channels(): pl.pallas_call(functools.partial(kernel, n, n_inner), out_shape=jax.Shape...  81.8 us
    unnamed x1, local copies, waits for them, and re-layouts  2.29 us

profile of v5, /device:TPU:1, one launch (start us, length us, event | category | flops | bytes accessed | tf_op | source)
XLA Modules:
  0.0 84.1 jit_solution(16964567393637435312)
XLA Ops:
  0.0 81.8 %shard_map.73 = bf16[128,4096]{1,0:T(8,128)(2,1)} custom-call(bf16[128,12288]{1,0:T(8,128)(2,1)} %proj_hbm.1, bf16[128,4096]{1,0:T(8,128)(2,1)} %filt_hbm.1, bf16[3,12288]{1,0:T(4,128)(2,1)} %taps_ref.1, f32[1,4096]{1,0:T(1,128)} %bitcast.1, bf16[256,256]{1,0:T(8,128)(2,1)} %constant.6.clone.fwd_ref, bf16[256,256]{1,0:T(8,128)(2,1)} %constant.7.clone.bwd_ref, ...), custom_call_target="tpu_custom_call" | custom-call | flops 1660944384 | bytes 5242880 | tf_op jit(solution)/shard_map/pallas_call | solution.py:431
  81.9 2.3 %copy.9 = bf16[128,4096]{1,0:T(8,128)(2,1)} copy(bf16[128,4096]{1,0:T(8,128)(2,1)} %shard_map.73) | data formatting | bytes 2097152

commit v6 on v5

--- a/solution.py
+++ b/solution.py
@@ -182,11 +182,11 @@
             return carry
         lax.fori_loop(0, n, run, 0)
 
-    def loop(count, body):
+    def loop(count, body, unroll=1):
         def run(step, carry):
             body(step)
             return carry
-        lax.fori_loop(0, count, run, 0)
+        lax.fori_loop(0, count, run, 0, unroll=unroll)
 
     def halo_copy(to):
         return pltpu.make_async_remote_copy(
@@ -227,6 +227,13 @@
         last = tail[:, block * LANES:(block + 1) * LANES].astype(jnp.float32)
         halo[2 * block:2 * block + 2, :] = last[ROWS - 2:]
     halo_out[...] = halo[...].astype(jnp.bfloat16)
+
+    left = lax.broadcasted_iota(jnp.int32, (half_tok, LANES), 1) < HALF
+    for freq in range(freqs):
+        for part in range(2):
+            column = turn_ref[part][:, freq:freq + 1]
+            turn[freq, part] = jnp.where(left, column[:half_tok], column[half_tok:])
+    first[quads - 1] = jnp.zeros(first.shape[1:], first.dtype)
 
     load_filt.wait()
     pl.semaphore_wait(barrier, n - 1)
@@ -287,13 +294,6 @@
     each_partner(start_gate)
     gate_in[0, me], gate_in[1, me] = make_gate(me)
     each_partner(lambda to, number: send_filter(1, to, number))
-
-    left = lax.broadcasted_iota(jnp.int32, (half_tok, LANES), 1) < HALF
-    for freq in range(freqs):
-        for part in range(2):
-            column = turn_ref[part][:, freq:freq + 1]
-            turn[freq, part] = jnp.where(left, column[:half_tok], column[half_tok:])
-    first[quads - 1] = jnp.zeros(first.shape[1:], first.dtype)
 
     def spot(tile, shift):
         return pl.ds(pl.multiple_of(shift + tile * ROWS, ROWS), ROWS)
@@ -396,7 +396,7 @@
             conv_in[0, block].astype(jnp.float32), conv_in[1, block].astype(jnp.float32)), 0)
         out_ref[:, cols] = (query[block] * rows + direct[block]).astype(jnp.bfloat16)
 
-    loop(n, finish)
+    loop(n, finish, unroll=4)
 
     @pl.when(me < n - 1)
     def _():

time: 84.3 us -> 82.6 us (0.980)
  Pallas kernels: 81.8 us -> 80.1 us
    pallas_call x1, Pallas kernels: 81.8 us -> 80.1 us  [by_channels(): pl.pallas_call(functools.partial(kernel, n, n_inner), out_shape=jax.Shape...]
where the time goes in v6:
time: 82.6 us; the launch traced here: 82.4 us
  Pallas kernels  80.1 us (97%)
  local copies, waits for them, and re-layouts  2.29 us (3%)
    pallas_call x1, Pallas kernels, by_channels(): pl.pallas_call(functools.partial(kernel, n, n_inner), out_shape=jax.Shape...  80.1 us
    unnamed x1, local copies, waits for them, and re-layouts  2.29 us

profile of v6, /device:TPU:1, one launch (start us, length us, event | category | flops | bytes accessed | tf_op | source)
XLA Modules:
  0.0 82.4 jit_solution(5849090884450759199)
XLA Ops:
  0.0 80.1 %shard_map.73 = bf16[128,4096]{1,0:T(8,128)(2,1)} custom-call(bf16[128,12288]{1,0:T(8,128)(2,1)} %proj_hbm.1, bf16[128,4096]{1,0:T(8,128)(2,1)} %filt_hbm.1, bf16[3,12288]{1,0:T(4,128)(2,1)} %taps_ref.1, f32[1,4096]{1,0:T(1,128)} %bitcast.1, bf16[256,256]{1,0:T(8,128)(2,1)} %constant.6.clone.fwd_ref, bf16[256,256]{1,0:T(8,128)(2,1)} %constant.7.clone.bwd_ref, ...), custom_call_target="tpu_custom_call" | custom-call | flops 1660944384 | bytes 5242880 | tf_op jit(solution)/shard_map/pallas_call | solution.py:431
  80.1 2.3 %copy.9 = bf16[128,4096]{1,0:T(8,128)(2,1)} copy(bf16[128,4096]{1,0:T(8,128)(2,1)} %shard_map.73) | data formatting | bytes 2097152
